TPU v7x, 128 devices: a whole 4x4x4 slice. The times are simulated.
128 devices in a mesh: row: 16 (over y, x), col: 8 (over z, core).
Axes of the slice: x: 4, y: 4, z: 4, core: 2. Of those that a mesh axis runs over, the one named last changes fastest.
Arguments:
- upper_block: float32 [2, 1024, 1024], P(None, 'row', 'col'), may hold values from -0.25 to 0.25
- block_inverse: float32 [2, 1024, 64], P(None, 'row'), may hold values from -0.375 to 0.375
- panel_rhs: float32 [2, 32, 1024], P(None, None, 'row'), may hold values from -6 to 6
- upper_trail: float32 [2, 1024, 131072], P(None, 'row', 'col'), may hold values from -0.125 to 0.125
- trail_rhs: float32 [2, 32, 131072], P(None, None, ('col', 'row')), may hold values from -6 to 6
- currents: float32 [2, 1024], P(None, 'row'), may hold values from -4 to 4
- owner: int32 [1024], P('row'), may hold values from 0 to 511
Outputs:
- panel_adjoint: float32 [2, 32, 1024], P(None, None, 'row')
- trail_updated: float32 [2, 32, 131072], P(None, None, ('col', 'row'))
- patch_gradient: float32 [512], P(('row', 'col'))
Inputs may be any that keep to these rules, and one draw needn't show every extreme that they name: owner names a surface patch for each panel unknown.
All inputs are finite; a program needn't handle non-finite values.
Results may differ from a plain program's by a relative error of at most 0.0003.
Values sent between devices are 32-bit elements; how exact they have to be, the bound alone decides.
A program may use at most 64 MiB of HBM per device.

v0:
```python
import jax
import jax.numpy as jnp
from jax import lax
from jax.sharding import Mesh
from jax.sharding import PartitionSpec as P

PATCH_DEV = 4
ROW = ("row_0", "row_1")
ROW_COL = ("row_0", "row_1", "col")
COL_ROW = ("col", "row_0", "row_1")
highest = lax.Precision.HIGHEST


def rows_first(arrays, axis, dims):
    turned = [jnp.moveaxis(a, dim, 0) for a, dim in zip(arrays, dims)]
    widths = [t[0].size for t in turned]
    both = jnp.concatenate([t.reshape(-1, w) for t, w in zip(turned, widths)], axis=1)
    filled = lax.all_gather(both, axis, axis=0, tiled=True)
    pieces = jnp.split(filled, [sum(widths[:k]) for k in range(1, len(widths))], axis=1)
    return tuple(
        (
            jnp.moveaxis(b.reshape(-1, *t.shape[1:]), 0, dim)
            for b, t, dim in zip(pieces, turned, dims)
        )
    )


def sum_by_axis(value, axes, dim):
    if not axes:
        return value
    nearer = lax.psum_scatter(value, axes[0], scatter_dimension=dim, tiled=True)
    return sum_by_axis(nearer, axes[1:], dim)


def product_high(first, second):
    return jnp.dot(first, second, precision=highest, preferred_element_type=jnp.float32)


def conj_product(left, right):
    real_part = product_high(left[0], right[0]) + product_high(left[1], right[1])
    imag_part = product_high(left[1], right[0]) - product_high(left[0], right[1])
    return jnp.stack([real_part, imag_part])


def sweep(upper, inverses, rhs, width):
    count = rhs.shape[2] // width
    held_start = jnp.zeros(rhs.shape, jnp.float32)
    solved_start = jnp.zeros(rhs.shape, jnp.float32)

    def advance(index, carry):
        held, solved = carry
        start = (jnp.asarray(index) * width).astype(jnp.int32)
        local = lax.dynamic_slice_in_dim(held, start, width, 2)
        residual = lax.dynamic_slice_in_dim(rhs, start, width, 2) - local
        inverse = lax.dynamic_slice_in_dim(inverses, start, width, 1)
        value = conj_product(residual, inverse)
        rows_here = lax.dynamic_slice_in_dim(upper, start, width, 1)
        held = held + conj_product(value, rows_here)
        solved = lax.dynamic_update_slice_in_dim(solved, value, start, 2)
        return (held, solved)

    return lax.fori_loop(0, count, advance, (held_start, solved_start))[1]


def on_device(upper_block, block_inverse, panel_rhs, upper_trail, trail_rhs, currents, owner):
    rows_count = lax.axis_size(ROW)
    cols_count = lax.axis_size("col")
    row_index = lax.axis_index(ROW)
    col_index = lax.axis_index("col")
    width = block_inverse.shape[1]
    whole_rows, inverses, rhs_all = rows_first(
        (upper_block, block_inverse, panel_rhs), ROW, (1, 1, 2)
    )
    whole = lax.all_gather(whole_rows, "col", axis=2, tiled=True)
    solved_all = sweep(whole, inverses, rhs_all, width)
    solved = lax.dynamic_slice_in_dim(solved_all, row_index * width, width, 2)
    term = conj_product(solved, upper_trail)
    reduced = sum_by_axis(term, ROW, 2)
    updated = trail_rhs - reduced
    share = width // cols_count
    start = col_index * share
    mine = lax.dynamic_slice_in_dim(solved, start, share, 2)
    total = jnp.sum(mine, axis=1)
    current_part = lax.dynamic_slice_in_dim(currents, start, share, 1)
    owner_part = lax.dynamic_slice_in_dim(owner, start, share, 0)
    partial_value = current_part[0] * total[0] - current_part[1] * total[1]
    patch_count = PATCH_DEV * rows_count * cols_count
    patch_ids = lax.broadcasted_iota(jnp.int32, (share, patch_count), 1)
    selector = (owner_part[:, None] == patch_ids).astype(jnp.float32)
    spread = product_high(partial_value[None, :], selector)[0]
    gradient = lax.psum_scatter(spread, ROW_COL, scatter_dimension=0, tiled=True)
    return (solved, updated, gradient)


def solution(mesh):
    split = Mesh(mesh.devices.reshape(4, 4, mesh.shape["col"]), ("row_0", "row_1", "col"))
    return jax.shard_map(
        on_device,
        mesh=split,
        in_specs=(
            P(None, ROW, "col"),
            P(None, ROW, None),
            P(None, None, ROW),
            P(None, ROW, "col"),
            P(None, None, COL_ROW),
            P(None, ROW),
            P(ROW),
        ),
        out_specs=(P(None, None, ROW), P(None, None, COL_ROW), P(ROW_COL)),
        check_vma=False,
    )
```

profile of v0, /device:TPU:1, one launch (start us, length us, event | category | flops | bytes accessed | tf_op | source)
XLA Modules:
  0.0 364.6 jit_solution(3339413474390331940)
XLA Ops:
  9.8 48.1 %all-gather.3.cloned.1.call-done = f32[1024,448]{1,0:T(8,128)} async-done(((f32[64,448]{1,0:T(8,128)}), f32[1024,448]{1,0:T(8,128)}) %all-gather.3.cloned.1.call-update) | async-done | bytes 1835024 | tf_op jit(solution)/shard_map/all_gather | solution.py:18
  57.9 1.4 split.14
  59.3 1.3 copy.31
  61.2 50.3 %all-gather.5.cloned.1.call-done = f32[2,1024,1024]{1,2,0:T(8,128)} async-done(((f32[2,1024,128]{1,2,0:T(8,128)}), f32[2,1024,1024]{1,2,0:T(8,128)}) %all-gather.5.cloned.1.call-update) | async-done | bytes 8388624 | tf_op jit(solution)/shard_map/all_gather | solution.py:74
  111.4 8.7 %copy.33 = f32[2,1024,1024]{2,1,0:T(8,128)} copy(f32[2,1024,1024]{1,2,0:T(8,128)} %all-gather.5.cloned.1.call-done) | data formatting | bytes 16777216
  120.1 106.3 %while.16 = (s32[]{:T(128)}, f32[2,32,1024]{2,1,0:T(8,128)S(1)}, f32[2,32,1024]{2,1,0:T(8,128)S(1)}, f32[2,32,1024]{2,1,0:T(8,128)S(1)}, f32[2,1024,64]{1,2,0:T(...) while((s32[]{:T(128)}, f32[2,32,1024]{2,1,0:T(8,128)S(1)}, ...), condition=%wide.region_1.0_spmd.clone, body=%wide.region_0.0_spmd.clone.sunk | while | flops 107294728 | bytes 3555570 | solution.py:62
  120.8 1.2 fusion.58
  122.5 1.2 fusion.60
  127.3 1.2 fusion.58
  129.0 1.2 fusion.60
  131.4 1.2 fusion.62
  134.1 1.2 fusion.58
  135.8 1.2 fusion.60
  138.2 1.2 fusion.62
  140.6 1.2 fusion.58
  142.3 1.2 fusion.60
  147.4 1.2 fusion.58
  149.1 1.2 fusion.60
  151.6 1.2 fusion.62
  155.6 1.2 fusion.60
  158.1 1.2 fusion.62
  160.7 1.2 fusion.58
  162.4 1.2 fusion.60
  164.9 1.2 fusion.62
  167.2 1.2 fusion.58
  168.9 1.2 fusion.60
  175.7 1.2 fusion.60
  178.2 1.2 fusion.62
  182.2 1.2 fusion.60
  187.3 1.2 fusion.58
  189.0 1.2 fusion.60
  195.5 1.2 fusion.60
  198.0 1.2 fusion.62
  202.3 1.2 fusion.60
  207.1 1.2 fusion.58
  208.8 1.2 fusion.60
  215.6 1.2 fusion.60
  218.1 1.2 fusion.62
  222.1 1.2 fusion.60
  224.5 1.2 fusion.62
  226.4 4.0 %fusion.20 = f32[32,16384]{1,0:T(8,128)S(1)} fusion(f32[2,64,16384]{2,1,0:T(8,128)} %param.12, f32[2,32,1024]{2,1,0:T(8,128)S(1)} %get-tuple-element.112, s32[]{:T(128)S(6)} %select_n.23), kind=kOutput, calls=%fused_computation.37 | convolution fusion | flops 402653184 | bytes 6307844 | tf_op jit(solution)/shard_map/dot_general | solution.py:36
  230.5 4.0 %fusion.18 = f32[32,16384]{1,0:T(8,128)S(1)} fusion(f32[2,64,16384]{2,1,0:T(8,128)} %param.12, f32[2,32,1024]{2,1,0:T(8,128)S(1)} %get-tuple-element.112, s32[]{:T(128)S(6)} %add.84, s32[]{:T(128)S(6)} %select_n.23), kind=kOutput, calls=%fused_computation.35 | convolution fusion | flops 402653184 | bytes 6307848 | tf_op jit(solution)/shard_map/dot_general | solution.py:36
  234.5 3.9 %fusion.14 = f32[1,32,16384]{2,1,0:T(8,128)S(1)} fusion(f32[32,16384]{1,0:T(8,128)S(1)} %fusion.18, f32[2,64,16384]{2,1,0:T(8,128)} %param.12, f32[2,32,1024]{2,1,0:T(8,128)S(1)} %get-tuple-element.112, s32[]{:T(128)S(6)} %select_n.23), kind=kOutput, calls=%fused_computation.29 | convolution fusion | flops 403177472 | bytes 8404996 | tf_op jit(solution)/shard_map/dot_general | solution.py:36
  238.5 2.2 fusion.15
  240.7 2.2 pad_maximum_fusion.1
  243.0 46.6 %reduce-scatter.3.cloned.1.call-done = f32[2,32,4096]{2,1,0:T(8,128)} async-done(((f32[2,32,16384]{2,1,0:T(8,128)}), f32[2,32,4096]{2,1,0:T(8,128)}) %reduce-scatter.3.cloned.1.call-update) | async-done | bytes 1048592 | tf_op jit(solution)/shard_map/reduce_scatter | solution.py:31
  290.1 65.0 %all-reduce = f32[512]{0:T(512)S(1)} all-reduce(f32[512]{0:T(512)S(1)} %bitcast.133), channel_id=4, replica_groups=mesh['row_0'=4,'row_1'=4,'col'=8] {'row_0','row_1','col'}, use_global_device_ids=true, to_apply=%region_5.0.clone | all-reduce | flops 512 | bytes 4096
  356.4 1.7 sub.32
  (215 shorter events, 67.6 us)
Async XLA Ops:
  7.2 1.9 copy-start
  7.2 50.8 %all-gather.3.cloned.1.call-start = ((), (), s32[]{:S(2)}) async-start(), calls=%async_computation.2 | async-start | bytes 2228224 | tf_op jit(solution)/shard_map/all_gather | solution.py:18
  9.8 101.7 %all-gather.5.cloned.1.call-start = ((), (), s32[]{:S(2)}) async-start(), calls=%async_computation.3 | async-start | bytes 9437184 | tf_op jit(solution)/shard_map/all_gather | solution.py:74
  57.9 2.8 slice-start.2
  57.9 3.0 slice-start.3
  60.7 228.9 %reduce-scatter.3.cloned.1.call-start = ((), (), s32[]{:S(2)}) async-start(), calls=%async_computation.4 | async-start | bytes 5242880 | tf_op jit(solution)/shard_map/reduce_scatter | solution.py:31
  226.4 12.1 %slice-start = ((s8[8388608]{0:T(1024)(128)(4,1)}), s8[4194304]{0:T(1024)(128)(4,1)S(1)}, s32[]{:S(2)}) async-start(s8[8388608]{0:T(1024)(128)(4,1)} %bitcast.124), calls=%async_computation.6 | async-start | bytes 8388608
  230.5 8.0 %slice-start.1 = ((s8[8388608]{0:T(1024)(128)(4,1)}), s8[4194304]{0:T(1024)(128)(4,1)S(1)}, s32[]{:S(2)}) async-start(s8[8388608]{0:T(1024)(128)(4,1)} %bitcast.124), calls=%async_computation.7 | async-start | bytes 8388608
  242.9 46.7 %copy-start.3 = (s32[64]{0:T(128)S(1)}, s32[64]{0:T(128)}, u32[]{:S(2)}) copy-start(s32[64]{0:T(128)} %param.15) | copy-start | bytes 772
  242.9 46.8 %copy-start.2 = (f32[2,64]{1,0:T(2,128)S(1)}, f32[2,64]{1,0:T(2,128)}, u32[]{:S(2)}) copy-start(f32[2,64]{1,0:T(2,128)} %param.14) | copy-start | bytes 1540
  242.9 113.4 %copy-start.1 = (f32[2,32,1024]{2,1,0:T(8,128)S(1)}, f32[2,32,1024]{2,1,0:T(8,128)}, u32[]{:S(2)}) copy-start(f32[2,32,1024]{2,1,0:T(8,128)} %param.13) | copy-start | bytes 786436
  243.0 113.4 %reduce-scatter.5.cloned.1.call-start = ((), (), s32[]{:S(2)}) async-start(), calls=%async_computation.5 | async-start | bytes 1310720 | tf_op jit(solution)/shard_map/reduce_scatter | solution.py:31
Sparse Core Ops, SparseCore 0:
  10.7 47.1 all-gather.2
  60.8 50.5 all-gather.4
  243.1 46.4 reduce-scatter.2
  292.0 20.9 reduce-scatter.4
where the time goes:
time: 367 us; the launch traced here: 365 us
  waiting for transfers between devices  145 us (40%)
  matrix products  108 us (29%)
  blocking collectives  65 us (18%)
  local copies, waits for them, and re-layouts  22.7 us (6%)
  between operations  13.9 us (4%)
  other arithmetic  7.86 us (2%)
    dot_general x133, matrix products, product_high(): jnp.dot(first, second, precision=highest, preferred_element_type=jnp.floa...  108 us
    unnamed x1, blocking collectives  65 us
    all_gather x1, waiting for transfers between devices, on_device(): whole = lax.all_gather(whole_rows, 'col', axis=2, tiled=True)  50.3 us
    all_gather x1, waiting for transfers between devices, rows_first(): filled = lax.all_gather(both, axis, axis=0, tiled=True)  48.1 us
    reduce_scatter x2, waiting for transfers between devices, sum_by_axis(): nearer = lax.psum_scatter(value, axes[0], scatter_dimension=dim, tiled=True)  46.6 us
    unnamed x14, local copies, waits for them, and re-layouts  9.29 us
    dynamic_update_slice x16, local copies, waits for them, and re-layouts, advance(): solved = lax.dynamic_update_slice_in_dim(solved, value, start, 2)  7.65 us
  transfers between devices with their start and end apart: 4, of which 3 were waited for; matrix products, arithmetic and copies ran while one was open for 1% of the time, Pallas kernels for 0%

commit v1 on v0

--- a/solution.py
+++ b/solution.py
@@ -71,7 +71,16 @@
     whole_rows, inverses, rhs_all = rows_first(
         (upper_block, block_inverse, panel_rhs), ROW, (1, 1, 2)
     )
-    whole = lax.all_gather(whole_rows, "col", axis=2, tiled=True)
+    ways = lax.axis_size("col")
+    up = [(d, (d + 1) % ways) for d in range(ways)]
+    down = [(d, (d - 1) % ways) for d in range(ways)]
+    earlier, later = ([whole_rows], [whole_rows])
+    for _ in range(ways // 2):
+        earlier.append(lax.ppermute(earlier[-1], "col", up))
+    for _ in range((ways - 1) // 2):
+        later.append(lax.ppermute(later[-1], "col", down))
+    line = jnp.concatenate([*earlier[::-1], *later[1:]], axis=2)
+    whole = jnp.roll(line, (lax.axis_index("col") - ways // 2) * whole_rows.shape[2], axis=2)
     solved_all = sweep(whole, inverses, rhs_all, width)
     solved = lax.dynamic_slice_in_dim(solved_all, row_index * width, width, 2)
     term = conj_product(solved, upper_trail)

time: 367 us -> 459 us (1.25); the launches traced: 365 us -> 450 us
  matrix products: 108 us -> 156 us
  local copies, waits for them, and re-layouts: 22.7 us -> 45.5 us
  starting transfers between devices: 0.16 us -> 13.3 us
  other arithmetic: 7.86 us -> 20 us
  waiting for transfers between devices: 145 us -> 134 us
    all_gather x1 -> x0, waiting for transfers between devices: 50.3 us -> none  [on_device(): whole = lax.all_gather(whole_rows, 'col', axis=2, tiled=True)]
    dot_general x133, matrix products: 108 us -> 156 us  [product_high(): jnp.dot(first, second, precision=highest, preferred_element_type=jnp.floa...]
    ppermute x0 -> x7, waiting for transfers between devices: none -> 36.6 us  [the longest x4 35.7 us: on_device(): earlier.append(lax.ppermute(earlier[-1], 'col', up))]
    ppermute x0 -> x7, starting transfers between devices: none -> 13.2 us  [the longest x4 10.2 us: on_device(): earlier.append(lax.ppermute(earlier[-1], 'col', up))]
    sub x16, other arithmetic: 1.42 us -> 13.5 us  [advance(): residual = lax.dynamic_slice_in_dim(rhs, start, width, 2) - local]
    unnamed x14 -> x35, local copies, waits for them, and re-layouts: 9.29 us -> 20.4 us
    split x8 -> x6, local copies, waits for them, and re-layouts: 3.09 us -> 9.35 us  [rows_first(): jnp.split(filled, [sum(widths[:k]) for k in range(1, len(widths))], axis=1)]
  transfers between devices with their start and end apart: 4 -> 10, of which waited for: 3 -> 8; matrix products, arithmetic and copies ran while one was open for 1% -> 3% of each run, Pallas kernels for 0% -> 0%
where the time goes in v1:
time: 459 us; the launch traced here: 450 us
  matrix products  156 us (34%)
  waiting for transfers between devices  134 us (29%)
  blocking collectives  64.9 us (14%)
  local copies, waits for them, and re-layouts  45.5 us (10%)
  other arithmetic  20 us (4%)
  between operations  14 us (3%)
  starting transfers between devices  13.3 us (3%)
    dot_general x133, matrix products, product_high(): jnp.dot(first, second, precision=highest, preferred_element_type=jnp.floa...  156 us
    unnamed x1, blocking collectives  64.9 us
    reduce_scatter x2, waiting for transfers between devices, sum_by_axis(): nearer = lax.psum_scatter(value, axes[0], scatter_dimension=dim, tiled=True)  49.3 us
    all_gather x1, waiting for transfers between devices, rows_first(): filled = lax.all_gather(both, axis, axis=0, tiled=True)  48.1 us
    ppermute x4, waiting for transfers between devices, on_device(): earlier.append(lax.ppermute(earlier[-1], 'col', up))  35.7 us
    unnamed x35, local copies, waits for them, and re-layouts  20.4 us
    sub x16, other arithmetic, advance(): residual = lax.dynamic_slice_in_dim(rhs, start, width, 2) - local  13.5 us
    ppermute x4, starting transfers between devices, on_device(): earlier.append(lax.ppermute(earlier[-1], 'col', up))  10.2 us
  transfers between devices with their start and end apart: 10, of which 8 were waited for; matrix products, arithmetic and copies ran while one was open for 3% of the time, Pallas kernels for 0%

profile of v1, /device:TPU:1, one launch (start us, length us, event | category | flops | bytes accessed | tf_op | source)
XLA Modules:
  0.0 450.1 jit_solution(11181216800083650599)
XLA Ops:
  9.8 48.1 %all-gather.2.cloned.1.call-done = f32[1024,448]{1,0:T(8,128)} async-done(((f32[64,448]{1,0:T(8,128)}), f32[1024,448]{1,0:T(8,128)}) %all-gather.2.cloned.1.call-update) | async-done | bytes 1835024 | tf_op jit(solution)/shard_map/all_gather | solution.py:18
  57.9 1.3 split.14
  59.6 2.7 collective-permute-start
  62.2 11.7 %collective-permute-done = f32[2,1024,128]{1,2,0:T(8,128)S(1)} collective-permute-done((f32[2,1024,128]{1,2,0:T(8,128)S(1)}, f32[2,1024,128]{1,2,0:T(8,128)S(1)}, u32[]{:S(2)}, u32[]{:S(2)}) %collective-permute-start) | collective-permute-done | bytes 1048608 | tf_op jit(solution)/shard_map/ppermute | solution.py:79
  74.0 2.5 collective-permute-start.1
  76.5 11.7 %collective-permute-done.1 = f32[2,1024,128]{1,2,0:T(8,128)S(1)} collective-permute-done((f32[2,1024,128]{1,2,0:T(8,128)S(1)}, f32[2,1024,128]{1,2,0:T(8,128)S(1)}, u32[]{:S(2)}, u32[]{:S(2)}) %collective-permute-start.1) | collective-permute-done | bytes 1048608 | tf_op jit(solution)/shard_map/ppermute | solution.py:79
  88.2 2.5 collective-permute-start.2
  92.0 10.5 %collective-permute-done.2 = f32[2,1024,128]{1,2,0:T(8,128)} collective-permute-done((f32[2,1024,128]{1,2,0:T(8,128)S(1)}, f32[2,1024,128]{1,2,0:T(8,128)}, u32[]{:S(2)}, u32[]{:S(2)}) %collective-permute-start.2) | collective-permute-done | bytes 1048608 | tf_op jit(solution)/shard_map/ppermute | solution.py:79
  102.4 2.6 collective-permute-start.3
  105.6 1.9 collective-permute-start.6
  107.5 1.9 split.12
  109.4 1.9 copy.29
  111.3 1.9 split.13
  113.2 2.0 copy.30
  115.3 1.8 collective-permute-done.3
  117.1 1.3 constant_dynamic-update-slice_fusion.15
  118.4 1.3 constant_dynamic-update-slice_fusion.14
  119.7 1.3 constant_dynamic-update-slice_fusion.13
  121.3 1.3 constant_dynamic-update-slice_fusion.9
  122.6 1.3 constant_dynamic-update-slice_fusion.8
  123.9 1.3 constant_dynamic-update-slice_fusion.7
  125.2 1.3 constant_dynamic-update-slice_fusion.6
  127.0 1.3 constant_dynamic-update-slice_fusion.1
  128.3 1.3 constant_dynamic-update-slice_fusion
  129.6 4.1 constant_dynamic-slice_fusion.2
  133.7 8.7 %copy.33 = f32[2,1024,1024]{2,1,0:T(8,128)} copy(f32[2,1024,1024]{1,2,0:T(8,128)} %constant_dynamic-slice_fusion.2) | data formatting | bytes 16777216
  142.4 166.8 %while.16 = (s32[]{:T(128)}, f32[2,32,1024]{2,1,0:T(8,128)S(1)}, f32[2,32,1024]{2,1,0:T(8,128)S(1)}, f32[2,32,1024]{2,1,0:T(8,128)}, f32[2,1024,64]{1,2,0:T(8,12...) while((s32[]{:T(128)}, f32[2,32,1024]{2,1,0:T(8,128)S(1)}, ...), condition=%wide.region_1.2_spmd.clone, body=%wide.region_0.1_spmd.clone.sunk | while | flops 107294728 | bytes 3555570 | solution.py:62
  148.6 1.2 fusion.60
  158.9 1.2 fusion.60
  169.4 1.2 fusion.60
  179.7 1.2 fusion.60
  190.3 1.2 fusion.60
  200.6 1.2 fusion.60
  211.2 1.2 fusion.60
  221.5 1.2 fusion.60
  232.0 1.2 fusion.60
  242.3 1.2 fusion.60
  252.9 1.2 fusion.60
  263.2 1.2 fusion.60
  284.1 1.2 fusion.60
  309.2 4.0 fusion.20
  313.3 4.0 fusion.18
  317.4 3.9 fusion.14
  321.4 2.2 fusion.15
  323.6 2.2 pad_maximum_fusion.1
  325.9 49.3 %reduce-scatter.3.cloned.1.call-done = f32[2,32,4096]{2,1,0:T(8,128)} async-done(((f32[2,32,16384]{2,1,0:T(8,128)}), f32[2,32,4096]{2,1,0:T(8,128)}) %reduce-scatter.3.cloned.1.call-update) | async-done | bytes 1048592 | tf_op jit(solution)/shard_map/reduce_scatter | solution.py:31
  375.7 64.9 %all-reduce = f32[512]{0:T(512)S(1)} all-reduce(f32[512]{0:T(512)S(1)} %bitcast.136), channel_id=4, replica_groups=mesh['row_0'=4,'row_1'=4,'col'=8] {'row_0','row_1','col'}, use_global_device_ids=true, to_apply=%region_5.6.clone | all-reduce | flops 512 | bytes 4096
  441.9 1.7 sub.41
  (247 shorter events, 156.1 us)
Async XLA Ops:
  7.2 1.9 copy-start
  7.2 50.8 %all-gather.2.cloned.1.call-start = ((), (), s32[]{:S(2)}) async-start(), calls=%async_computation.2 | async-start | bytes 2228224 | tf_op jit(solution)/shard_map/all_gather | solution.py:18
  9.8 365.4 %reduce-scatter.3.cloned.1.call-start = ((), (), s32[]{:S(2)}) async-start(), calls=%async_computation.3 | async-start | bytes 5242880 | tf_op jit(solution)/shard_map/reduce_scatter | solution.py:31
  59.6 14.4 %collective-permute-start = (f32[2,1024,128]{1,2,0:T(8,128)S(1)}, f32[2,1024,128]{1,2,0:T(8,128)S(1)}, u32[]{:S(2)}, u32[]{:S(2)}) collective-permute-start(f32[2,1024,128]{1,2,0:T(8,128)S(1)} %bitcast.126), channel_id=1, source_target_pairs={{0,1},{1,2},{2,3},{3,4},{4,5},{5,6},{6,7},{7,0},{8,9},{9,10},{10,1... | collective-permute-start | bytes 3145736 | tf_op jit(solution)/shard_map/ppermute | solution.py:79
  74.0 14.2 %collective-permute-start.1 = (f32[2,1024,128]{1,2,0:T(8,128)S(1)}, f32[2,1024,128]{1,2,0:T(8,128)S(1)}, u32[]{:S(2)}, u32[]{:S(2)}) collective-permute-start(f32[2,1024,128]{1,2,0:T(8,128)S(1)} %collective-permute-done), channel_id=1, source_target_pairs={{0,1},{1,2},{2,3},{3,4},{4,5},{5,6},{6,7},{7,0},{8,9},{9,10},{10,1... | collective-permute-start | bytes 3145736 | tf_op jit(solution)/shard_map/ppermute | solution.py:79
  76.5 14.5 %collective-permute-start.4 = (f32[2,1024,128]{1,2,0:T(8,128)S(1)}, f32[2,1024,128]{1,2,0:T(8,128)S(1)}, u32[]{:S(2)}, u32[]{:S(2)}) collective-permute-start(f32[2,1024,128]{1,2,0:T(8,128)S(1)} %bitcast.127), channel_id=1, source_target_pairs={{0,7},{1,0},{2,1},{3,2},{4,3},{5,4},{6,5},{7,6},{8,15},{9,8},{10,9... | collective-permute-start | bytes 3145736 | tf_op jit(solution)/shard_map/ppermute | solution.py:81
  88.2 17.4 %copy-start.2 = (f32[2,1024,128]{1,2,0:T(8,128)}, f32[2,1024,128]{1,2,0:T(8,128)S(1)}, u32[]{:S(2)}) copy-start(f32[2,1024,128]{1,2,0:T(8,128)S(1)} %collective-permute-done.1) | copy-start | bytes 3145732
  88.2 14.2 %collective-permute-start.2 = (f32[2,1024,128]{1,2,0:T(8,128)S(1)}, f32[2,1024,128]{1,2,0:T(8,128)}, u32[]{:S(2)}, u32[]{:S(2)}) collective-permute-start(f32[2,1024,128]{1,2,0:T(8,128)S(1)} %collective-permute-done.1), channel_id=1, source_target_pairs={{0,1},{1,2},{2,3},{3,4},{4,5},{5,6},{6,7},{7,0},{8,9},{9,10},{10,1... | collective-permute-start | bytes 3145736 | tf_op jit(solution)/shard_map/ppermute | solution.py:79
  91.0 14.6 %collective-permute-start.5 = (f32[2,1024,128]{1,2,0:T(8,128)S(1)}, f32[2,1024,128]{1,2,0:T(8,128)}, u32[]{:S(2)}, u32[]{:S(2)}) collective-permute-start(f32[2,1024,128]{1,2,0:T(8,128)S(1)} %collective-permute-done.4), channel_id=1, source_target_pairs={{0,7},{1,0},{2,1},{3,2},{4,3},{5,4},{6,5},{7,6},{8,15},{9,8},{10,9... | collective-permute-start | bytes 3145736 | tf_op jit(solution)/shard_map/ppermute | solution.py:81
  102.4 14.6 %collective-permute-start.3 = (f32[2,1024,128]{1,2,0:T(8,128)}, f32[2,1024,128]{1,2,0:T(8,128)}, u32[]{:S(2)}, u32[]{:S(2)}) collective-permute-start(f32[2,1024,128]{1,2,0:T(8,128)} %collective-permute-done.2), channel_id=1, source_target_pairs={{0,1},{1,2},{2,3},{3,4},{4,5},{5,6},{6,7},{7,0},{8,9},{9,10},{10,1... | collective-permute-start | bytes 3145736 | tf_op jit(solution)/shard_map/ppermute | solution.py:79
  105.6 17.0 %collective-permute-start.6 = (f32[2,1024,128]{1,2,0:T(8,128)}, f32[2,1024,128]{1,2,0:T(8,128)}, u32[]{:S(2)}, u32[]{:S(2)}) collective-permute-start(f32[2,1024,128]{1,2,0:T(8,128)} %collective-permute-done.5), channel_id=1, source_target_pairs={{0,7},{1,0},{2,1},{3,2},{4,3},{5,4},{6,5},{7,6},{8,15},{9,8},{10,9... | collective-permute-start | bytes 3145736 | tf_op jit(solution)/shard_map/ppermute | solution.py:81
  115.3 11.3 %copy-start.3 = (f32[2,1024,128]{1,2,0:T(8,128)S(1)}, f32[2,1024,128]{1,2,0:T(8,128)}, u32[]{:S(2)}) copy-start(f32[2,1024,128]{1,2,0:T(8,128)} %copy-done.2) | copy-start | bytes 3145732
  309.2 12.1 %slice-start = ((s8[8388608]{0:T(1024)(128)(4,1)}), s8[4194304]{0:T(1024)(128)(4,1)S(1)}, s32[]{:S(2)}) async-start(s8[8388608]{0:T(1024)(128)(4,1)} %bitcast.124), calls=%async_computation.5 | async-start | bytes 8388608
  313.3 8.1 %slice-start.1 = ((s8[8388608]{0:T(1024)(128)(4,1)}), s8[4194304]{0:T(1024)(128)(4,1)S(1)}, s32[]{:S(2)}) async-start(s8[8388608]{0:T(1024)(128)(4,1)} %bitcast.124), calls=%async_computation.6 | async-start | bytes 8388608
  313.3 130.3 %copy-start.1 = (f32[2,64,128]{2,1,0:T(8,128)S(1)}, f32[2,64,128]{2,1,0:T(8,128)}, u32[]{:S(2)}) copy-start(f32[2,64,128]{2,1,0:T(8,128)} %param.9) | copy-start | bytes 196612
  317.4 57.9 %copy-start.6 = (s32[64]{0:T(128)S(1)}, s32[64]{0:T(128)}, u32[]{:S(2)}) copy-start(s32[64]{0:T(128)} %param.15) | copy-start | bytes 772
  317.4 58.0 %copy-start.5 = (f32[2,64]{1,0:T(2,128)S(1)}, f32[2,64]{1,0:T(2,128)}, u32[]{:S(2)}) copy-start(f32[2,64]{1,0:T(2,128)} %param.14) | copy-start | bytes 1540
  317.4 124.5 %copy-start.4 = (f32[2,32,1024]{2,1,0:T(8,128)S(1)}, f32[2,32,1024]{2,1,0:T(8,128)}, u32[]{:S(2)}) copy-start(f32[2,32,1024]{2,1,0:T(8,128)} %param.13) | copy-start | bytes 786436
  325.8 116.0 %reduce-scatter.5.cloned.1.call-start = ((), (), s32[]{:S(2)}) async-start(), calls=%async_computation.4 | async-start | bytes 1310720 | tf_op jit(solution)/shard_map/reduce_scatter | solution.py:31
Sparse Core Ops, SparseCore 0:
  10.7 47.1 all-gather.1
  326.0 49.1 reduce-scatter.2
  377.7 21.8 reduce-scatter.4
